TPU v7x, 128 devices: a whole 4x4x4 slice. The times are simulated.
128 devices in a mesh: bulk: 32 (over x, z, core), contact: 4 (over y).
Axes of the slice: x: 4, y: 4, z: 4, core: 2. Of those that a mesh axis runs over, the one named last changes fastest.
Arguments:
- k_inv: float32 [262144, 2048], P(('bulk', 'contact'))
- mortar_slave: float32 [32768, 256], P(('bulk', 'contact')), may hold values from -0.375 to 0.375
- mortar_master: float32 [32768, 256], P(('bulk', 'contact')), may hold values from -0.375 to 0.375
- force: float32 [262144, 256], P(('bulk', 'contact')), may hold values from -6 to 6
- lam_glue: float32 [32768, 256], P(('bulk', 'contact')), may hold values from -6 to 6
- lam_contact: float32 [32768, 256], P(('bulk', 'contact')), may hold values from 0 to 1
- master_map: int32 [128], P(('bulk', 'contact')), may hold values from 0 to 3, as said below
- on_surface: int32 [128], P(('bulk', 'contact')), may hold values 0 or 1
- step_type: int32 [2, 256], replicated, may hold values from 0 to 2
- active: int32 [2, 32768, 256], P(None, ('bulk', 'contact')), may hold values 0 or 1
- expand_len: float32 [256], replicated, may hold values from 0.05 to 0.3
Outputs:
- glue_final: float32 [32768, 256], P(('bulk', 'contact'))
- contact_final: float32 [32768, 256], P(('bulk', 'contact'))
- grad_glue_final: float32 [32768, 256], P(('bulk', 'contact'))
- grad_contact_final: float32 [32768, 256], P(('bulk', 'contact'))
Inputs may be any that keep to these rules, and one draw needn't show every extreme that they name: master_map never names the subdomain's own position in its group of 4.
All inputs are finite; a program needn't handle non-finite values. No bound on the sum of `on_surface` or of `active` on one device may be relied on, other than what follows from the above.
Results may differ from a plain program's by a relative error of at most 0.0003.
Values sent between devices are 32-bit elements; how exact they have to be, the bound alone decides.
No kernel may reach another device: no remote copies, remote signals or barrier semaphores. Data moves between devices by JAX's collectives and lax.ppermute only.
A program may use at most 128 MiB of HBM per device.

v0:
```python
import jax
import jax.numpy as jnp
from jax import lax
from jax.sharding import PartitionSpec as P

precise = lax.Precision.HIGHEST


def passed_along(value, axis, steps):
    count = lax.axis_size(axis)
    leading, last = (max(0, -steps), min(count, count - steps))
    return lax.ppermute(value, axis, [(source, source + steps) for source in range(leading, last)])


def local_inner(first_glue, first_contact, second_glue, second_contact):
    return jnp.sum(first_glue * second_glue, axis=0) + jnp.sum(
        first_contact * second_contact, axis=0
    )


def per_device(
    k_inv,
    mortar_slave,
    mortar_master,
    force,
    lam_glue,
    lam_contact,
    master_map,
    on_surface,
    step_type,
    active,
    expand_len,
):
    face_rows = lam_glue.shape[0]
    mortar_rows = lam_contact.shape[0]
    columns = lam_glue.shape[1]
    order = k_inv.shape[0]
    group_size = lax.axis_size("contact")
    glue_mask = (lax.axis_index("bulk") < lax.axis_size("bulk") - 1).astype(jnp.float32)
    surface = on_surface[0].astype(jnp.float32)
    master_pick = (jnp.arange(group_size, dtype=jnp.int32) == master_map[0]).astype(jnp.float32)

    def operate(glue_dual, contact_dual, primal_load):
        previous = passed_along(glue_dual, "bulk", 1)
        slave_term = jnp.dot(mortar_slave.T, contact_dual, precision=precise) * surface
        outgoing = (
            master_pick[:, None, None]
            * (jnp.dot(mortar_master.T, contact_dual, precision=precise) * surface)[None]
        )
        received = lax.psum_scatter(outgoing, "contact", scatter_dimension=0, tiled=True)[0]
        interior = jnp.zeros((order - 2 * face_rows - mortar_rows, columns), jnp.float32)
        pushed = (
            jnp.concatenate([-previous, glue_dual, slave_term - received, interior], axis=0)
            - primal_load
        )
        response = jnp.dot(k_inv, pushed, precision=precise)
        following = passed_along(response[:face_rows], "bulk", -1)
        glue_out = (response[face_rows : 2 * face_rows] - following) * glue_mask
        contact_face = response[2 * face_rows : 2 * face_rows + mortar_rows]
        faces = lax.all_gather(contact_face[None], "contact", axis=0, tiled=True)
        master_face = jnp.einsum("t,tcr->cr", master_pick, faces, precision=precise)
        master_gap = jnp.dot(mortar_master, master_face, precision=precise)
        contact_out = (
            jnp.dot(mortar_slave, contact_face, precision=precise) - master_gap
        ) * surface
        return (glue_out, contact_out)

    glue_now = lam_glue * glue_mask
    contact_now = lam_contact
    grad_glue, grad_contact = operate(glue_now, contact_now, force)
    prev_glue = jnp.zeros_like(glue_now)
    prev_contact = jnp.zeros_like(contact_now)
    prev_image_glue = jnp.zeros_like(glue_now)
    prev_image_contact = jnp.zeros_like(contact_now)
    curvature = jnp.ones((columns,), jnp.float32)
    for sweep in range(step_type.shape[0]):
        active_now = active[sweep].astype(jnp.float32)
        kinds = step_type[sweep]
        is_cg = (kinds == 0).astype(jnp.float32)
        is_expand = (kinds == 1).astype(jnp.float32)
        is_chop = (kinds == 2).astype(jnp.float32)
        free_glue = grad_glue
        free_contact = grad_contact * (1.0 - active_now) * surface
        chopped = jnp.minimum(grad_contact, 0.0) * active_now * surface
        if sweep > 0:
            conj_ratio = (
                lax.psum(
                    local_inner(free_glue, free_contact, prev_image_glue, prev_image_contact),
                    ("bulk", "contact"),
                )
                / curvature
            )
        else:
            conj_ratio = jnp.zeros((columns,), jnp.float32)
        keep = is_cg + is_expand
        dir_glue = keep * free_glue - is_cg * conj_ratio * prev_glue
        dir_contact = keep * free_contact - is_cg * conj_ratio * prev_contact + is_chop * chopped
        descent = lax.psum(
            local_inner(grad_glue, grad_contact, dir_glue, dir_contact), ("bulk", "contact")
        )
        image_glue, image_contact = operate(dir_glue, dir_contact, 0.0)
        curvature = lax.psum(
            local_inner(dir_glue, dir_contact, image_glue, image_contact), ("bulk", "contact")
        )
        step_len = jnp.where(kinds == 1, expand_len, descent / curvature)
        half_glue = glue_now - step_len * dir_glue
        half_contact = contact_now - step_len * dir_contact
        correction = is_expand * surface * jnp.maximum(-half_contact, 0.0)
        fix_glue, fix_contact = operate(jnp.zeros_like(half_glue), correction, 0.0)
        glue_now = half_glue
        contact_now = half_contact + correction
        grad_glue = grad_glue - step_len * image_glue + fix_glue
        grad_contact = grad_contact - step_len * image_contact + fix_contact
        prev_glue, prev_contact = (dir_glue, dir_contact)
        prev_image_glue, prev_image_contact = (image_glue, image_contact)
    return (glue_now, contact_now, grad_glue, grad_contact)


def solution(mesh):
    placed = (
        P(("bulk", "contact"), None),
        P(("bulk", "contact"), None),
        P(("bulk", "contact"), None),
        P(("bulk", "contact"), None),
        P(("bulk", "contact"), None),
        P(("bulk", "contact"), None),
        P(("bulk", "contact")),
        P(("bulk", "contact")),
        P(),
        P(None, ("bulk", "contact"), None),
        P(),
    )
    return jax.shard_map(
        per_device,
        mesh=mesh,
        in_specs=placed,
        out_specs=(
            P(("bulk", "contact"), None),
            P(("bulk", "contact"), None),
            P(("bulk", "contact"), None),
            P(("bulk", "contact"), None),
        ),
        check_vma=False,
    )
```

profile of v0, /device:TPU:1, one launch (start us, length us, event | category | flops | bytes accessed | tf_op | source)
XLA Modules:
  0.0 657.2 jit_solution(6236599709612080260)
XLA Ops:
  12.6 4.9 collective-permute-start
  24.6 12.6 %reduce-scatter.6.cloned.1.call-done = f32[1,256,256]{1,2,0:T(8,128)} async-done(((f32[4,256,256]{1,2,0:T(8,128)}), f32[1,256,256]{1,2,0:T(8,128)}) %reduce-scatter.6.cloned.1.call-update) | async-done | bytes 262160 | tf_op jit(solution)/shard_map/reduce_scatter | solution.py:50
  40.6 31.2 %convolution_bitcast_fusion.4 = f32[2048,256]{0,1:T(8,128)S(1)} fusion(f32[2048,2048]{1,0:T(8,128)} %param.11, f32[2048,256]{1,0:T(8,128)S(1)} %copy-done.2, f32[256,256]{1,0:T(8,128)S(1)} %copy.20, f32[256,256]{1,0:T(8,128)S(1)} %copy.19, f32[256,256]{1,0:T(8,128)} %copy.18, f32[2048]{0:T(1024)S(1)} %pad.19.clone), kind=kOutput, calls=%fused_computation.4 | convolution fusion | flops 12886999040 | bytes 21766144 | tf_op jit(solution)/shard_map/dot_general | solution.py:56
  75.9 4.1 collective-permute-start.1
  81.3 16.8 %all-gather.11.cloned.1.call-done = f32[1024,256]{0,1:T(8,128)} async-done(((f32[256,256]{0,1:T(8,128)}), f32[1024,256]{0,1:T(8,128)}) %all-gather.11.cloned.1.call-update) | async-done | bytes 1048592 | tf_op jit(solution)/shard_map/all_gather | solution.py:60
  104.3 4.6 collective-permute-start.2
  113.1 14.7 %reduce-scatter.8.cloned.1.call-done = f32[1,256,256]{1,2,0:T(8,128)} async-done(((f32[4,256,256]{1,2,0:T(8,128)}), f32[1,256,256]{1,2,0:T(8,128)}) %reduce-scatter.8.cloned.1.call-update) | async-done | bytes 262160 | tf_op jit(solution)/shard_map/reduce_scatter | solution.py:50
  129.9 30.9 %convolution_bitcast_fusion.3 = f32[2048,256]{0,1:T(8,128)S(1)} fusion(f32[2048,2048]{1,0:T(8,128)} %param.11, f32[256,256]{1,0:T(8,128)} %copy.28, f32[256,256]{1,0:T(8,128)} %copy.27, f32[256,256]{1,0:T(8,128)} %copy.26, f32[2048]{0:T(1024)S(1)} %pad.19.clone), kind=kOutput, calls=%fused_computation.3 | convolution fusion | flops 12886474752 | bytes 19668992 | tf_op jit(solution)/shard_map/dot_general | solution.py:56
  161.8 4.0 collective-permute-start.3
  168.6 2.6 collective-permute-done.3
  173.0 13.0 %all-gather.13.cloned.1.call-done = f32[1024,256]{0,1:T(8,128)} async-done(((f32[256,256]{0,1:T(8,128)}), f32[1024,256]{0,1:T(8,128)}) %all-gather.13.cloned.1.call-update) | async-done | bytes 1048592 | tf_op jit(solution)/shard_map/all_gather | solution.py:60
  190.3 65.7 %all-reduce.1 = (f32[256]{0:T(256)S(1)}, f32[256]{0:T(256)S(1)}) all-reduce(f32[256]{0:T(256)S(1)} %add.69, f32[256]{0:T(256)S(1)} %add.70), channel_id=1, replica_groups=mesh['bulk'=32,'contact'=4] {'bulk','contact'}, use_global_device_ids=true, to_apply=%region_3.0 | all-reduce | flops 512 | bytes 4096 | tf_op jit(solution)/shard_map/psum | solution.py:98
  257.8 2.5 collective-permute-start.4
  260.3 3.3 collective-permute-done.4
  264.4 12.3 %reduce-scatter.10.cloned.1.call-done = f32[1,256,256]{1,2,0:T(8,128)} async-done(((f32[4,256,256]{1,2,0:T(8,128)}), f32[1,256,256]{1,2,0:T(8,128)}) %reduce-scatter.10.cloned.1.call-update) | async-done | bytes 262160 | tf_op jit(solution)/shard_map/reduce_scatter | solution.py:50
  278.9 31.9 %convolution_bitcast_fusion.2 = f32[2048,256]{0,1:T(8,128)S(1)} fusion(f32[2048,2048]{1,0:T(8,128)} %param.11, f32[256,256]{1,0:T(8,128)} %copy.34, f32[256,256]{1,0:T(8,128)} %copy.32, f32[2048]{0:T(1024)S(1)} %pad.9.clone, f32[2048]{0:T(1024)S(1)} %pad.19.clone), kind=kOutput, calls=%fused_computation.2 | convolution fusion | flops 12886474752 | bytes 19415040 | tf_op jit(solution)/shard_map/dot_general | solution.py:56
  311.7 3.9 collective-permute-start.5
  318.6 2.6 collective-permute-done.5
  323.0 12.9 %all-gather.15.cloned.1.call-done = f32[1024,256]{0,1:T(8,128)} async-done(((f32[256,256]{0,1:T(8,128)}), f32[1024,256]{0,1:T(8,128)}) %all-gather.15.cloned.1.call-update) | async-done | bytes 1048592 | tf_op jit(solution)/shard_map/all_gather | solution.py:60
  340.7 65.7 %psum.37 = f32[256]{0:T(256)S(1)} all-reduce(f32[256]{0:T(256)S(1)} %add.74), channel_id=1, replica_groups=mesh['bulk'=32,'contact'=4] {'bulk','contact'}, use_global_device_ids=true, to_apply=%region_11.12 | all-reduce | flops 256 | bytes 2048 | tf_op jit(solution)/shard_map/psum | solution.py:87
  415.8 12.2 %reduce-scatter.12.cloned.1.call-done = f32[1,256,256]{1,2,0:T(8,128)} async-done(((f32[4,256,256]{1,2,0:T(8,128)}), f32[1,256,256]{1,2,0:T(8,128)}) %reduce-scatter.12.cloned.1.call-update) | async-done | bytes 262160 | tf_op jit(solution)/shard_map/reduce_scatter | solution.py:50
  430.2 30.9 %convolution_bitcast_fusion.1 = f32[2048,256]{0,1:T(8,128)S(1)} fusion(f32[2048,2048]{1,0:T(8,128)} %param.11, f32[256,256]{1,0:T(8,128)} %copy.42, f32[256,256]{1,0:T(8,128)} %copy.41, f32[256,256]{1,0:T(8,128)} %copy.40, f32[2048]{0:T(1024)S(1)} %pad.19.clone), kind=kOutput, calls=%fused_computation.1 | convolution fusion | flops 12886474752 | bytes 19668992 | tf_op jit(solution)/shard_map/dot_general | solution.py:56
  462.0 4.0 collective-permute-start.7
  467.1 4.3 collective-permute-done.7
  473.4 13.0 %all-gather.17.cloned.1.call-done = f32[1024,256]{0,1:T(8,128)} async-done(((f32[256,256]{0,1:T(8,128)}), f32[1024,256]{0,1:T(8,128)}) %all-gather.17.cloned.1.call-update) | async-done | bytes 1048592 | tf_op jit(solution)/shard_map/all_gather | solution.py:60
  486.4 2.7 reshape.35
  489.1 3.0 fusion.90
  496.3 65.6 %all-reduce = (f32[256]{0:T(256)S(1)}, f32[256]{0:T(256)S(1)}) all-reduce(f32[256]{0:T(256)S(1)} %add.76, f32[256]{0:T(256)S(1)} %add.77), channel_id=1, replica_groups=mesh['bulk'=32,'contact'=4] {'bulk','contact'}, use_global_device_ids=true, to_apply=%region_14.15 | all-reduce | flops 512 | bytes 4096 | tf_op jit(solution)/shard_map/psum | solution.py:98
  565.1 18.9 %reduce-scatter.14.cloned.1.call-done = f32[1,256,256]{1,2,0:T(8,128)} async-done(((f32[4,256,256]{1,2,0:T(8,128)}), f32[1,256,256]{1,2,0:T(8,128)}) %reduce-scatter.14.cloned.1.call-update) | async-done | bytes 262160 | tf_op jit(solution)/shard_map/reduce_scatter | solution.py:50
  587.2 31.8 %convolution_bitcast_fusion = f32[2048,256]{0,1:T(8,128)S(1)} fusion(f32[2048,2048]{1,0:T(8,128)} %param.11, f32[256,256]{1,0:T(8,128)S(1)} %copy-done.11, f32[256,256]{1,0:T(8,128)S(1)} %copy.47, f32[2048]{0:T(1024)S(1)} %pad.9.clone, f32[2048]{0:T(1024)S(1)} %pad.19.clone), kind=kOutput, calls=%fused_computation | convolution fusion | flops 12886474752 | bytes 19415040 | tf_op jit(solution)/shard_map/dot_general | solution.py:56
  621.2 4.0 collective-permute-start.8
  635.4 10.2 %all-gather.19.cloned.1.call-done = f32[1024,256]{0,1:T(8,128)} async-done(((f32[256,256]{0,1:T(8,128)}), f32[1024,256]{0,1:T(8,128)}) %all-gather.19.cloned.1.call-update) | async-done | bytes 1048592 | tf_op jit(solution)/shard_map/all_gather | solution.py:60
  (173 shorter events, 99.8 us)
Async XLA Ops:
  7.2 30.0 %reduce-scatter.6.cloned.1.call-start = ((), (), s32[]{:S(2)}) async-start(), calls=%async_computation.5 | async-start | bytes 1310720 | tf_op jit(solution)/shard_map/reduce_scatter | solution.py:50
  11.6 25.6 %copy-start.1 = (f32[256,256]{1,0:T(8,128)S(1)}, f32[256,256]{1,0:T(8,128)}, u32[]{:S(2)}) copy-start(f32[256,256]{1,0:T(8,128)} %param.12) | copy-start | bytes 786436
  11.6 25.6 %copy-start.17 = (f32[256,256]{1,0:T(8,128)S(1)}, f32[256,256]{1,0:T(8,128)}, u32[]{:S(2)}) copy-start(f32[256,256]{1,0:T(8,128)} %param.16) | copy-start | bytes 786436
  11.6 86.5 %all-gather.11.cloned.1.call-start = ((), (), s32[]{:S(2)}) async-start(), calls=%async_computation.10 | async-start | bytes 1310720 | tf_op jit(solution)/shard_map/all_gather | solution.py:60
  11.7 28.9 %copy-start.2 = (f32[2048,256]{1,0:T(8,128)S(1)}, f32[2048,256]{1,0:T(8,128)}, u32[]{:S(2)}) copy-start(f32[2048,256]{1,0:T(8,128)} %param.14) | copy-start | bytes 6291460
  11.9 59.9 %copy-start.14 = (f32[256,256]{0,1:T(8,128)}, f32[256,256]{0,1:T(8,128)S(1)}, u32[]{:S(2)}) copy-start(f32[256,256]{0,1:T(8,128)S(1)} %copy.15) | copy-start | bytes 786436
  12.6 8.5 %collective-permute-start = (f32[256,256]{0,1:T(8,128)}, f32[256,256]{0,1:T(8,128)}, u32[]{:S(2)}, u32[]{:S(2)}) collective-permute-start(f32[256,256]{0,1:T(8,128)} %broadcast_multiply_fusion.6), channel_id=1, source_target_pairs={{0,4},{4,8},{8,12},{12,16},{16,20},{20,24},{24,28},{28,32},{32,36}... | collective-permute-start | bytes 786440 | tf_op jit(solution)/shard_map/ppermute | solution.py:12
  73.9 53.9 %reduce-scatter.8.cloned.1.call-start = ((), (), s32[]{:S(2)}) async-start(), calls=%async_computation.6 | async-start | bytes 1310720 | tf_op jit(solution)/shard_map/reduce_scatter | solution.py:50
  75.9 25.2 %collective-permute-start.1 = (f32[256,256]{0,1:T(8,128)S(1)}, f32[256,256]{0,1:T(8,128)S(1)}, u32[]{:S(2)}, u32[]{:S(2)}) collective-permute-start(f32[256,256]{0,1:T(8,128)S(1)} %get-tuple-element.39), channel_id=1, source_target_pairs={{4,0},{8,4},{12,8},{16,12},{20,16},{24,20},{28,24},{32,28},{36,32}... | collective-permute-start | bytes 786440 | tf_op jit(solution)/shard_map/ppermute | solution.py:12
  102.7 86.3 %copy-start.15 = (f32[256,256]{0,1:T(8,128)}, f32[256,256]{0,1:T(8,128)S(1)}, u32[]{:S(2)}) copy-start(f32[256,256]{0,1:T(8,128)S(1)} %get-tuple-element.56) | copy-start | bytes 786436
  104.3 81.8 %all-gather.13.cloned.1.call-start = ((), (), s32[]{:S(2)}) async-start(), calls=%async_computation.11 | async-start | bytes 1310720 | tf_op jit(solution)/shard_map/all_gather | solution.py:60
  104.3 8.0 %collective-permute-start.2 = (f32[256,256]{0,1:T(8,128)S(1)}, f32[256,256]{0,1:T(8,128)S(1)}, u32[]{:S(2)}, u32[]{:S(2)}) collective-permute-start(f32[256,256]{0,1:T(8,128)S(1)} %get-tuple-element.28), channel_id=1, source_target_pairs={{0,4},{4,8},{8,12},{12,16},{16,20},{20,24},{24,28},{28,32},{32,36}... | collective-permute-start | bytes 786440 | tf_op jit(solution)/shard_map/ppermute | solution.py:12
  161.7 115.0 %reduce-scatter.10.cloned.1.call-start = ((), (), s32[]{:S(2)}) async-start(), calls=%async_computation.7 | async-start | bytes 1310720 | tf_op jit(solution)/shard_map/reduce_scatter | solution.py:50
  161.8 9.5 %collective-permute-start.3 = (f32[256,256]{0,1:T(8,128)}, f32[256,256]{0,1:T(8,128)}, u32[]{:S(2)}, u32[]{:S(2)}) collective-permute-start(f32[256,256]{0,1:T(8,128)} %get-tuple-element.37), channel_id=1, source_target_pairs={{4,0},{8,4},{12,8},{16,12},{20,16},{24,20},{28,24},{32,28},{36,32}... | collective-permute-start | bytes 786440 | tf_op jit(solution)/shard_map/ppermute | solution.py:12
  173.0 16.0 %copy-start.23 = (f32[256,256]{1,0:T(8,128)S(1)}, f32[256,256]{1,0:T(8,128)}, u32[]{:S(2)}) copy-start(f32[256,256]{1,0:T(8,128)} %fusion.123) | copy-start | bytes 786436
  187.7 68.2 %copy-start.26 = (f32[256]{0:T(256)S(1)}, f32[256]{0:T(256)}, u32[]{:S(2)}) copy-start(f32[256]{0:T(256)} %param.21) | copy-start | bytes 3076
  187.7 68.2 %copy-start.22 = (f32[256,256]{0,1:T(8,128)S(1)}, f32[256,256]{0,1:T(8,128)}, u32[]{:S(2)}) copy-start(f32[256,256]{0,1:T(8,128)} %copy.31) | copy-start | bytes 786436
  257.7 78.3 %all-gather.15.cloned.1.call-start = ((), (), s32[]{:S(2)}) async-start(), calls=%async_computation.12 | async-start | bytes 1310720 | tf_op jit(solution)/shard_map/all_gather | solution.py:60
  257.8 5.8 collective-permute-start.4
  311.7 116.4 %reduce-scatter.12.cloned.1.call-start = ((), (), s32[]{:S(2)}) async-start(), calls=%async_computation.8 | async-start | bytes 1310720 | tf_op jit(solution)/shard_map/reduce_scatter | solution.py:50
  311.7 9.5 %collective-permute-start.5 = (f32[256,256]{0,1:T(8,128)}, f32[256,256]{0,1:T(8,128)}, u32[]{:S(2)}, u32[]{:S(2)}) collective-permute-start(f32[256,256]{0,1:T(8,128)} %get-tuple-element.35), channel_id=1, source_target_pairs={{4,0},{8,4},{12,8},{16,12},{20,16},{24,20},{28,24},{32,28},{36,32}... | collective-permute-start | bytes 786440 | tf_op jit(solution)/shard_map/ppermute | solution.py:12
  323.0 15.9 %copy-start.18 = (s32[1,256,256]{1,2,0:T(8,128)S(1)}, s32[1,256,256]{1,2,0:T(8,128)}, u32[]{:S(2)}) copy-start(s32[1,256,256]{1,2,0:T(8,128)} %copy.66) | copy-start | bytes 786436
  337.7 68.7 %copy-start.5 = (f32[256,256]{0,1:T(8,128)S(1)}, f32[256,256]{0,1:T(8,128)}, u32[]{:S(2)}) copy-start(f32[256,256]{0,1:T(8,128)} %get-tuple-element.26) | copy-start | bytes 786436
  340.6 68.5 %copy-start.9 = (f32[256,256]{0,1:T(8,128)}, f32[256,256]{0,1:T(8,128)S(1)}, u32[]{:S(2)}) copy-start(f32[256,256]{0,1:T(8,128)S(1)} %get-tuple-element.59) | copy-start | bytes 786436
  409.1 77.3 %all-gather.17.cloned.1.call-start = ((), (), s32[]{:S(2)}) async-start(), calls=%async_computation.13 | async-start | bytes 1310720 | tf_op jit(solution)/shard_map/all_gather | solution.py:60
  409.2 5.8 collective-permute-start.6
  462.0 122.1 %reduce-scatter.14.cloned.1.call-start = ((), (), s32[]{:S(2)}) async-start(), calls=%async_computation.9 | async-start | bytes 1310720 | tf_op jit(solution)/shard_map/reduce_scatter | solution.py:50
  462.0 9.4 %collective-permute-start.7 = (f32[256,256]{0,1:T(8,128)}, f32[256,256]{0,1:T(8,128)S(1)}, u32[]{:S(2)}, u32[]{:S(2)}) collective-permute-start(f32[256,256]{0,1:T(8,128)} %get-tuple-element.33), channel_id=1, source_target_pairs={{4,0},{8,4},{12,8},{16,12},{20,16},{24,20},{28,24},{32,28},{36,32}... | collective-permute-start | bytes 786440 | tf_op jit(solution)/shard_map/ppermute | solution.py:12
  563.9 20.2 %copy-start.13 = (f32[256,256]{0,1:T(8,128)S(1)}, f32[256,256]{0,1:T(8,128)}, u32[]{:S(2)}) copy-start(f32[256,256]{0,1:T(8,128)} %copy-done.12) | copy-start | bytes 786436
  563.9 23.3 %copy-start.11 = (f32[256,256]{1,0:T(8,128)S(1)}, f32[256,256]{1,0:T(8,128)}, u32[]{:S(2)}) copy-start(f32[256,256]{1,0:T(8,128)} %copy.32) | copy-start | bytes 786436
  565.1 80.5 %all-gather.19.cloned.1.call-start = ((), (), s32[]{:S(2)}) async-start(), calls=%async_computation.14 | async-start | bytes 1310720 | tf_op jit(solution)/shard_map/all_gather | solution.py:60
  621.2 9.5 %collective-permute-start.8 = (f32[256,256]{0,1:T(8,128)}, f32[256,256]{0,1:T(8,128)}, u32[]{:S(2)}, u32[]{:S(2)}) collective-permute-start(f32[256,256]{0,1:T(8,128)} %get-tuple-element.31), channel_id=1, source_target_pairs={{4,0},{8,4},{12,8},{16,12},{20,16},{24,20},{28,24},{32,28},{36,32}... | collective-permute-start | bytes 786440 | tf_op jit(solution)/shard_map/ppermute | solution.py:12
  (14 other events, 95.6 us)
Sparse Core Ops, SparseCore 0:
  11.8 25.4 reduce-scatter.5
  74.0 24.1 all-gather.10
  104.4 23.3 reduce-scatter.7
  161.8 24.1 all-gather.12
  257.8 18.8 reduce-scatter.9
  311.8 24.1 all-gather.14
  409.2 18.7 reduce-scatter.11
  462.1 24.2 all-gather.16
  565.2 18.7 reduce-scatter.13
  621.3 24.2 all-gather.18
where the time goes:
time: 666 us; the launch traced here: 657 us
  blocking collectives  197 us (30%)
  matrix products  190 us (29%)
  waiting for transfers between devices  159 us (24%)
  local copies, waits for them, and re-layouts  42.9 us (6%)
  starting transfers between devices  34.9 us (5%)
  other arithmetic  17.3 us (3%)
  between operations  16.6 us (2%)
    dot_general x5, matrix products, operate(): response = jnp.dot(k_inv, pushed, precision=precise)  157 us
    psum x2, blocking collectives, per_device(): lax.psum(local_inner(grad_glue, grad_contact, dir_glue, dir_contact), ('b...  131 us
    reduce_scatter x5, waiting for transfers between devices, operate(): lax.psum_scatter(outgoing, 'contact', scatter_dimension=0, tiled=True)[0]  70.7 us
    all_gather x5, waiting for transfers between devices, operate(): faces = lax.all_gather(contact_face[None], 'contact', axis=0, tiled=True)  66 us
    psum x1, blocking collectives, per_device(): lax.psum(local_inner(free_glue, free_contact, prev_image_glue, prev_image...  65.7 us
    ppermute x9, starting transfers between devices, passed_along(): lax.ppermute(value, axis, [(source, source + steps) for source in range(l...  34.5 us
    ppermute x9, waiting for transfers between devices, passed_along(): lax.ppermute(value, axis, [(source, source + steps) for source in range(l...  21.9 us
    unnamed x62, local copies, waits for them, and re-layouts  13.4 us
  transfers between devices with their start and end apart: 19, of which 18 were waited for; matrix products, arithmetic and copies ran while one was open for 6% of the time, Pallas kernels for 0%

commit v1 on v0

v1 whole, which is shorter than its diff:
```python
import jax
import jax.numpy as jnp
from jax import lax
from jax.sharding import PartitionSpec as P

three_pass = lax.Precision.HIGH
everyone = ("bulk", "contact")


def mul(left, right):
    return jnp.dot(left, right, precision=three_pass)


def mul_t(left, right):
    return lax.dot_general(left, right, (((0,), (0,)), ((), ())), precision=three_pass)


def along_bulk(value, steps):
    count = lax.axis_size("bulk")
    leading, last = (max(0, -steps), min(count, count - steps))
    return lax.ppermute(value, "bulk", [(s, s + steps) for s in range(leading, last)])


def from_block(value, offset):
    count = lax.axis_size("contact")
    return lax.ppermute(value, "contact", [((d + offset) % count, d) for d in range(count)])


def total(rows):
    k, n = rows.shape
    count = lax.axis_size("bulk") * lax.axis_size("contact")
    spread = jnp.broadcast_to(rows.reshape(1, k * n), (count, k * n))
    got = lax.all_to_all(spread, everyone, 0, 0, tiled=True)
    return jnp.sum(got, axis=0).reshape(k, n)


def col(value):
    return jnp.sum(value, axis=0, keepdims=True)


def per_device(
    k_inv,
    mortar_slave,
    mortar_master,
    force,
    lam_glue,
    lam_contact,
    master_map,
    on_surface,
    step_type,
    active,
    expand_len,
):
    f = lam_glue.shape[0]
    m = lam_contact.shape[0]
    n = lam_glue.shape[1]
    rows = 2 * f + m
    bulk_at = lax.axis_index("bulk")
    own_mask = (bulk_at < lax.axis_size("bulk") - 1).astype(jnp.float32)
    prev_mask = (bulk_at > 0).astype(jnp.float32)
    here = lax.axis_index("contact").astype(jnp.float32)
    surface = on_surface[0].astype(jnp.float32)
    slave = mortar_slave * surface
    master = mortar_master * surface
    note = jnp.broadcast_to(master_map[0].astype(jnp.float32), (8, n))
    active_f = active.astype(jnp.float32)

    first = jnp.concatenate([master, lam_contact, note], axis=0)
    first_r = from_block(first, 1)
    first_l = from_block(first, 3)
    far_master = from_block(first_l[:m], 3)
    far_lam = from_block(first_r[m:], 1)
    second = jnp.concatenate([slave, active_f[0]], axis=0)
    second, far_master, far_lam = lax.optimization_barrier((second, far_master, far_lam))
    second_r = from_block(second, 1)
    second_l = from_block(second, 3)
    far_slave = from_block(second_l[:m], 3)
    far_active = from_block(second_r[m:], 1)

    masters = jnp.concatenate([first_r[:m], far_master, first_l[:m]], axis=0)
    lam_c = jnp.concatenate([lam_contact, first_r[m : 2 * m], far_lam[:m], first_l[m : 2 * m]], axis=0)
    names = [
        (note_o == here).astype(jnp.float32)
        for note_o in (first_r[2 * m, 0], far_lam[m, 0], first_l[2 * m, 0])
    ]
    own_master = master_map[0].astype(jnp.float32)
    picks = [
        (own_master == (lax.axis_index("contact") + o) % lax.axis_size("contact")).astype(jnp.float32)
        for o in (1, 2, 3)
    ]
    masters_named = jnp.concatenate(
        [masters[o * m : (o + 1) * m] * names[o] for o in range(3)], axis=0
    )
    slaves = [slave, second_r[:m], far_slave, second_l[:m]]
    act0 = jnp.concatenate([active_f[0], second_r[m:], far_active, second_l[m:]], axis=0)
    block_surface = jnp.concatenate(
        [jnp.broadcast_to(surface, (m, 1)), jnp.ones((3 * m, 1), jnp.float32)], axis=0
    )

    k_top = k_inv[:rows]
    k_small = k_top[:, :rows]
    base = mul(k_top, force)

    def push(contact):
        return mul_t(slave, contact[:m]) - mul_t(masters_named, contact[m:])

    def assemble(glue, contact):
        return jnp.concatenate([-glue[f:], glue[:f], push(contact)], axis=0)

    def glue_trade(y):
        return along_bulk(y[f : 2 * f], 1), along_bulk(y[:f], -1)

    def group(y):
        return [from_block(y, 1), from_block(y, 3), from_block(y, 2)]

    def gaps(y, traded, others):
        before, after = traded
        glue = jnp.concatenate(
            [(y[f : 2 * f] - after) * own_mask, (before - y[:f]) * prev_mask], axis=0
        )
        own = y[2 * f :]
        blocks = [others[0], others[2], others[1]]
        chosen = picks[0] * blocks[0] + picks[1] * blocks[1] + picks[2] * blocks[2]
        below = mul(masters, own)
        contact = jnp.concatenate(
            [mul(slave, own) - mul(master, chosen)]
            + [mul(slaves[o + 1], blocks[o]) - below[o * m : (o + 1) * m] for o in range(3)],
            axis=0,
        )
        return glue, contact

    expand = expand_len[None, :]
    kinds = [step_type[i][None, :] for i in range(2)]
    is_cg = [(t == 0).astype(jnp.float32) for t in kinds]
    is_expand = [(t == 1).astype(jnp.float32) for t in kinds]
    is_chop = [(t == 2).astype(jnp.float32) for t in kinds]

    lam_g = lam_glue * own_mask
    lam_prev = along_bulk(lam_g, 1)
    y = mul(k_small, assemble(jnp.concatenate([lam_g, lam_prev], axis=0), lam_c)) - base
    others = group(y[2 * f :])
    traded = glue_trade(y)
    grad_g, grad_c = gaps(y, traded, others)

    keep = is_cg[0] + is_expand[0]
    dir_g = keep * grad_g
    dir_c = keep * grad_c * (1.0 - act0) + is_chop[0] * jnp.minimum(grad_c, 0.0) * act0
    fix0 = is_expand[0] * jnp.maximum(expand * dir_c - lam_c, 0.0) * block_surface
    w_dir = assemble(dir_g, dir_c)
    y_dir = mul(k_small, w_dir)
    y_fix = mul(k_small[:, 2 * f :], push(fix0))
    y_sent = jnp.where(kinds[0] == 1, expand * y_dir - y_fix, y_dir)
    sums = jnp.concatenate(
        [
            col(w_dir * y_dir),
            col(grad_g[:f] * dir_g[:f]) + col(grad_c[:m] * dir_c[:m]),
            col(w_dir * y_fix),
        ],
        axis=0,
    )
    both = group(jnp.concatenate([y_sent[2 * f :], active_f[1]], axis=0))
    traded = glue_trade(y_sent)
    sums = total(sums)
    curv0, desc0, cross0 = sums[0:1], sums[1:2], sums[2:3]
    others = [v[:m] for v in both]
    act1 = jnp.concatenate([active_f[1], both[0][m:], both[2][m:], both[1][m:]], axis=0)
    step0 = jnp.where(kinds[0] == 1, expand, desc0 / curv0)
    scale0 = jnp.where(kinds[0] == 1, 1.0, step0)
    image_g, image_c = gaps(y_sent, traded, others)
    grad_g = grad_g - scale0 * image_g
    grad_c = grad_c - scale0 * image_c
    lam1_g = lam_g - step0 * dir_g[:f]
    lam1_c = lam_c - step0 * dir_c + fix0

    keep = is_cg[1] + is_expand[1]
    free_g = keep * grad_g
    free_c = keep * grad_c * (1.0 - act1) + is_chop[1] * jnp.minimum(grad_c, 0.0) * act1
    fix1 = is_expand[1] * jnp.maximum(expand * free_c - lam1_c, 0.0) * block_surface
    long1 = jnp.where(kinds[1] == 1, expand, 1.0)
    w_now = assemble(long1 * free_g, long1 * free_c - fix1)
    y_now = mul(k_small, w_now)
    first_sum = col(w_now * y_dir)
    sums = jnp.concatenate(
        [
            first_sum,
            first_sum + col(w_dir * y_now),
            col(w_now * y_now),
            col(grad_g[:f] * free_g[:f]) + col(grad_c[:m] * free_c[:m]),
        ],
        axis=0,
    )
    faces = jnp.concatenate([y_now[2 * f :], y_dir[2 * f :]], axis=0)
    others = group(faces)
    after = along_bulk(jnp.concatenate([y_now[:f], y_dir[:f]], axis=0), -1)
    sums = total(sums)
    left_over = desc0 - step0 * curv0 + is_expand[0] * cross0
    conj = is_cg[1] * sums[0:1] / curv0
    curv1 = sums[2:3] - conj * sums[1:2] + conj * conj * curv0
    desc1 = sums[3:4] - conj * left_over
    step1 = jnp.where(kinds[1] == 1, expand, desc1 / curv1)
    scale1 = jnp.where(kinds[1] == 1, 1.0, step1)

    chosen = picks[0] * others[0] + picks[1] * others[2] + picks[2] * others[1]
    glue_image = (
        (y_now[f : 2 * f] - conj * y_dir[f : 2 * f]) - (after[:f] - conj * after[f:])
    ) * own_mask
    contact_image = mul(slave, y_now[2 * f :] - conj * y_dir[2 * f :]) - mul(
        master, chosen[:m] - conj * chosen[m:]
    )
    glue_out = lam1_g - step1 * (free_g[:f] - conj * dir_g[:f])
    contact_out = lam1_c[:m] - step1 * (free_c[:m] - conj * dir_c[:m]) + fix1[:m]
    return (
        glue_out,
        contact_out,
        grad_g[:f] - scale1 * glue_image,
        grad_c[:m] - scale1 * contact_image,
    )


def solution(mesh):
    whole = P(("bulk", "contact"), None)
    flat = P(("bulk", "contact"))
    return jax.shard_map(
        per_device,
        mesh=mesh,
        in_specs=(
            whole, whole, whole, whole, whole, whole, flat, flat,
            P(), P(None, ("bulk", "contact"), None), P(),
        ),
        out_specs=(whole, whole, whole, whole),
        check_vma=False,
    )
```

time: 666 us -> 220 us (0.33); the launches traced: 657 us -> 219 us
  blocking collectives: 197 us -> 0 us
  matrix products: 190 us -> 41.6 us
  waiting for transfers between devices: 159 us -> 58.8 us
  starting transfers between devices: 34.9 us -> 63.5 us
  local copies, waits for them, and re-layouts: 42.9 us -> 17.5 us
  other arithmetic: 17.3 us -> 32.3 us
  between operations: 16.6 us -> 5.17 us
    psum x3 -> x0, blocking collectives: 197 us -> none  [the longest x2 131 us: per_device(): lax.psum(local_inner(grad_glue, grad_contact, dir_glue, dir_contact), ('b...]
    dot_general x30 -> x27, matrix products: 190 us -> 41.6 us  [the longest x19 34.9 us: mul(): return jnp.dot(left, right, precision=three_pass)]
    reduce_scatter x5 -> x0, waiting for transfers between devices: 70.7 us -> none  [operate(): lax.psum_scatter(outgoing, 'contact', scatter_dimension=0, tiled=True)[0]]
    all_gather x5 -> x0, waiting for transfers between devices: 66 us -> none  [operate(): faces = lax.all_gather(contact_face[None], 'contact', axis=0, tiled=True)]
    ppermute x9 -> x23, waiting for transfers between devices: 21.9 us -> 52.9 us  [the longest x17 52.9 us: from_block(): lax.ppermute(value, 'contact', [((d + offset) % count, d) for d in range(...]
    all_to_all x0 -> x2, starting transfers between devices: none -> 21.8 us  [total(): got = lax.all_to_all(spread, everyone, 0, 0, tiled=True)]
    unnamed x62 -> x117, local copies, waits for them, and re-layouts: 13.4 us -> 1.58 us
    all_gather x5 -> x0, local copies, waits for them, and re-layouts: 9.45 us -> none  [operate(): faces = lax.all_gather(contact_face[None], 'contact', axis=0, tiled=True)]
  transfers between devices with their start and end apart: 19 -> 25, of which waited for: 18 -> 9; matrix products, arithmetic and copies ran while one was open for 6% -> 23% of each run, Pallas kernels for 0% -> 0%
where the time goes in v1:
time: 220 us; the launch traced here: 219 us
  starting transfers between devices  63.5 us (29%)
  waiting for transfers between devices  58.8 us (27%)
  matrix products  41.6 us (19%)
  other arithmetic  32.3 us (15%)
  local copies, waits for them, and re-layouts  17.5 us (8%)
  between operations  5.17 us (2%)
    ppermute x17, waiting for transfers between devices, from_block(): lax.ppermute(value, 'contact', [((d + offset) % count, d) for d in range(...  52.9 us
    dot_general x19, matrix products, mul(): return jnp.dot(left, right, precision=three_pass)  34.9 us
    ppermute x17, starting transfers between devices, from_block(): lax.ppermute(value, 'contact', [((d + offset) % count, d) for d in range(...  22.9 us
    all_to_all x2, starting transfers between devices, total(): got = lax.all_to_all(spread, everyone, 0, 0, tiled=True)  21.8 us
    ppermute x6, starting transfers between devices, along_bulk(): lax.ppermute(value, 'bulk', [(s, s + steps) for s in range(leading, last)])  18.8 us
    dot_general x8, matrix products, mul_t(): lax.dot_general(left, right, (((0,), (0,)), ((), ())), precision=three_pass)  6.73 us
    all_to_all x2, waiting for transfers between devices, total(): got = lax.all_to_all(spread, everyone, 0, 0, tiled=True)  5.88 us
  transfers between devices with their start and end apart: 25, of which 9 were waited for; matrix products, arithmetic and copies ran while one was open for 23% of the time, Pallas kernels for 0%

profile of v1, /device:TPU:1, one launch (start us, length us, event | category | flops | bytes accessed | tf_op | source)
XLA Modules:
  0.0 218.8 jit_solution(8294905108939324121)
XLA Ops:
  5.1 2.1 collective-permute-start.2
  10.4 4.5 %collective-permute-start = (f32[256,256]{1,0:T(8,128)}, f32[256,256]{1,0:T(8,128)}, u32[]{:S(2)}, u32[]{:S(2)}) collective-permute-start(f32[256,256]{1,0:T(8,128)} %broadcast_multiply_fusion.7), channel_id=1, source_target_pairs={{0,4},{4,8},{8,12},{12,16},{16,20},{20,24},{24,28},{28,32},{32,36}... | collective-permute-start | bytes 786440 | tf_op jit(solution)/shard_map/ppermute | solution.py:21
  17.7 6.4 %fusion = f32[768,256]{1,0:T(8,128)} fusion(f32[2048,256]{1,0:T(8,128)S(1)} %copy-done, f32[2048,2048]{1,0:T(8,128)} %param.11), kind=kOutput, calls=%fused_computation | convolution fusion | flops 2415919104 | bytes 9175040 | tf_op jit(solution)/shard_map/dot_general | solution.py:11
  30.8 2.5 %collective-permute-start.4 = (f32[264,256]{1,0:T(8,128)}, f32[264,256]{1,0:T(8,128)}, u32[]{:S(2)}, u32[]{:S(2)}) collective-permute-start(f32[264,256]{1,0:T(8,128)} %slice.342), channel_id=1, source_target_pairs={{1,0},{2,1},{3,2},{0,3},{5,4},{6,5},{7,6},{4,7},{9,8},{10,9},{11,1... | collective-permute-start | bytes 811016 | tf_op jit(solution)/shard_map/ppermute | solution.py:26
  46.2 3.1 %fusion.17 = f32[768,256]{1,0:T(8,128)S(1)} fusion(f32[768,256]{1,0:T(8,128)} %fusion, f32[2048,2048]{1,0:T(8,128)} %param.11, f32[256,256]{1,0:T(8,128)S(1)} %convolution_subtract_fusion.12, f32[256,256]{1,0:T(8,128)} %broadcast_multiply_fusion.7, f32[256,256]{1,0:T(8,128)} %neg.9), kind=kOutput, calls=%fused_computation.12 | convolution fusion | flops 906559488 | bytes 4718592 | tf_op jit(solution)/shard_map/dot_general | solution.py:11
  51.3 3.6 %collective-permute-start.6 = (f32[256,256]{1,0:T(8,128)S(1)}, f32[256,256]{1,0:T(8,128)S(1)}, u32[]{:S(2)}, u32[]{:S(2)}) collective-permute-start(f32[256,256]{1,0:T(8,128)S(1)} %get-tuple-element.52), channel_id=1, source_target_pairs={{0,4},{4,8},{8,12},{12,16},{16,20},{20,24},{24,28},{28,32},{32,36}... | collective-permute-start | bytes 786440 | tf_op jit(solution)/shard_map/ppermute | solution.py:21
  55.2 2.8 %collective-permute-start.10 = (f32[512,256]{1,0:T(8,128)S(1)}, f32[512,256]{1,0:T(8,128)S(1)}, u32[]{:S(2)}, u32[]{:S(2)}) collective-permute-start(f32[512,256]{1,0:T(8,128)S(1)} %copy-done.55), channel_id=1, source_target_pairs={{1,0},{2,1},{3,2},{0,3},{5,4},{6,5},{7,6},{4,7},{9,8},{10,9},{11,1... | collective-permute-start | bytes 1572872 | tf_op jit(solution)/shard_map/ppermute | solution.py:26
  59.9 2.7 %collective-permute-start.7 = (f32[256,256]{1,0:T(8,128)S(1)}, f32[256,256]{1,0:T(8,128)S(1)}, u32[]{:S(2)}, u32[]{:S(2)}) collective-permute-start(f32[256,256]{1,0:T(8,128)S(1)} %get-tuple-element.50), channel_id=1, source_target_pairs={{1,0},{2,1},{3,2},{0,3},{5,4},{6,5},{7,6},{4,7},{9,8},{10,9},{11,1... | collective-permute-start | bytes 786440 | tf_op jit(solution)/shard_map/ppermute | solution.py:26
  64.2 14.5 %collective-permute-done.11 = f32[512,256]{1,0:T(8,128)S(1)} collective-permute-done((f32[512,256]{1,0:T(8,128)S(1)}, f32[512,256]{1,0:T(8,128)S(1)}, u32[]{:S(2)}, u32[]{:S(2)}) %collective-permute-start.11) | collective-permute-done | bytes 524320 | tf_op jit(solution)/shard_map/ppermute | solution.py:26
  78.9 2.9 %collective-permute-start.13 = (f32[256,256]{1,0:T(8,128)S(1)}, f32[256,256]{1,0:T(8,128)S(1)}, u32[]{:S(2)}, u32[]{:S(2)}) collective-permute-start(f32[256,256]{1,0:T(8,128)S(1)} %slice.356), channel_id=1, source_target_pairs={{1,0},{2,1},{3,2},{0,3},{5,4},{6,5},{7,6},{4,7},{9,8},{10,9},{11,1... | collective-permute-start | bytes 786440 | tf_op jit(solution)/shard_map/ppermute | solution.py:26
  81.8 2.5 %collective-permute-done.9 = f32[256,256]{1,0:T(8,128)S(1)} collective-permute-done((f32[256,256]{1,0:T(8,128)S(1)}, f32[256,256]{1,0:T(8,128)S(1)}, u32[]{:S(2)}, u32[]{:S(2)}) %collective-permute-start.9) | collective-permute-done | bytes 262176 | tf_op jit(solution)/shard_map/ppermute | solution.py:26
  85.3 4.1 %collective-permute-done.12 = f32[256,256]{1,0:T(8,128)S(1)} collective-permute-done((f32[256,256]{1,0:T(8,128)S(1)}, f32[256,256]{1,0:T(8,128)S(1)}, u32[]{:S(2)}, u32[]{:S(2)}) %collective-permute-start.12) | collective-permute-done | bytes 262176 | tf_op jit(solution)/shard_map/ppermute | solution.py:26
  94.7 4.0 %multiply_reduce_fusion.4 = (f32[256]{0:T(256)S(1)}, f32[256]{0:T(256)S(1)}, f32[768,256]{1,0:T(8,128)S(1)}, f32[768,256]{1,0:T(8,128)}) fusion(f32[256,256]{1,0:T(8,128)S(1)} %convolution_subtract_fusion.7, f32[256,256]{1,0:T(8,128)S(1)} %get-tuple-element.64, f32[256,256]{1,0:T(8,128)S(1)} %get-tuple-element.65, ...), kind=kOutput, calls=%fused_computation.63 | convolution fusion | flops 908131840 | bytes 6295040 | tf_op jit(solution)/shard_map/dot_general | solution.py:11
  99.7 2.4 %fusion.37 = f32[768,256]{1,0:T(8,128)} fusion(f32[256,256]{1,0:T(8,128)} %get-tuple-element.58, f32[256,256]{1,0:T(8,128)} %collective-permute-done.3, f32[256,256]{1,0:T(8,128)S(1)} %copy-done.32, f32[768,256]{1,0:T(8,128)S(1)} %get-tuple-element.38), kind=kOutput, calls=%fused_computation.64 | convolution fusion | flops 302383104 | bytes 1835008 | tf_op jit(solution)/shard_map/dot_general | solution.py:11
  102.2 2.2 %collective-permute-start.14 = (f32[256,256]{1,0:T(8,128)}, f32[256,256]{1,0:T(8,128)}, u32[]{:S(2)}, u32[]{:S(2)}) collective-permute-start(f32[256,256]{1,0:T(8,128)} %get-tuple-element.46), channel_id=1, source_target_pairs={{4,0},{8,4},{12,8},{16,12},{20,16},{24,20},{28,24},{32,28},{36,32}... | collective-permute-start | bytes 786440 | tf_op jit(solution)/shard_map/ppermute | solution.py:21
  104.5 3.3 %collective-permute-start.15 = (f32[256,256]{1,0:T(8,128)}, f32[256,256]{1,0:T(8,128)}, u32[]{:S(2)}, u32[]{:S(2)}) collective-permute-start(f32[256,256]{1,0:T(8,128)} %get-tuple-element.47), channel_id=1, source_target_pairs={{0,4},{4,8},{8,12},{12,16},{16,20},{20,24},{24,28},{28,32},{32,36}... | collective-permute-start | bytes 786440 | tf_op jit(solution)/shard_map/ppermute | solution.py:21
  108.8 10.1 %all-to-all-start = ((f32[128,1,768]{2,1,0:T(1,128)}), f32[128,1,768]{2,1,0:T(1,128)}, u32[]{:S(2)}, u32[]{:S(2)}) async-start(f32[128,1,768]{2,1,0:T(1,128)} %broadcast_in_dim.64), calls=%async_computation | async-start | bytes 786432 | tf_op jit(solution)/shard_map/all_to_all | solution.py:33
  120.9 2.1 fusion.117
  124.8 2.6 %collective-permute-start.16 = (f32[512,256]{1,0:T(8,128)}, f32[512,256]{1,0:T(8,128)}, u32[]{:S(2)}, u32[]{:S(2)}) collective-permute-start(f32[512,256]{1,0:T(8,128)} %pad_maximum_fusion.12), channel_id=1, source_target_pairs={{1,0},{2,1},{3,2},{0,3},{5,4},{6,5},{7,6},{4,7},{9,8},{10,9},{11,1... | collective-permute-start | bytes 1572872 | tf_op jit(solution)/shard_map/ppermute | solution.py:26
  128.6 2.8 %all-to-all-done = f32[128,1,768]{2,1,0:T(1,128)} async-done(((f32[128,1,768]{2,1,0:T(1,128)}), f32[128,1,768]{2,1,0:T(1,128)}, u32[]{:S(2)}, u32[]{:S(2)}) %all-to-all-start) | async-done | bytes 393248 | tf_op jit(solution)/shard_map/all_to_all | solution.py:33
  134.4 15.4 %collective-permute-done.16 = f32[512,256]{1,0:T(8,128)} collective-permute-done((f32[512,256]{1,0:T(8,128)}, f32[512,256]{1,0:T(8,128)}, u32[]{:S(2)}, u32[]{:S(2)}) %collective-permute-start.16) | collective-permute-done | bytes 524320 | tf_op jit(solution)/shard_map/ppermute | solution.py:26
  158.3 3.5 %multiply_subtract_fusion = (f32[1024,256]{1,0:T(8,128)S(1)}, f32[1024,256]{1,0:T(8,128)}, f32[1024,256]{1,0:T(8,128)}, f32[1024,256]{1,0:T(8,128)S(1)}, f32[1024,256]{1,0:T(8,128)S(1)}) fusion(f32[256]{0:T(256)S(1)} %bitcast.85, f32[1024]{0:T(1024)S(1)} %concatenate.74, f32[256]{0:T(256)S(1)} %copy-done.56, f32[256]{0:T(256)S(1)} %bitcast.95, ...), kind=kLoop, calls=%fused_computation.36 | loop fusion | flops 9437184 | bytes 10498048 | tf_op jit(solution)/shard_map/sub | solution.py:180
  163.0 3.7 %multiply_reduce_fusion.1 = (f32[256]{0:T(256)S(1)}, f32[256]{0:T(256)S(1)}, f32[256]{0:T(256)S(1)}, f32[768,256]{1,0:T(8,128)}) fusion(f32[256,256]{1,0:T(8,128)S(1)} %copy-done.15, f32[256,256]{1,0:T(8,128)S(1)} %copy-done.11, f32[256,256]{1,0:T(8,128)S(1)} %copy-done.13, f32[256,256]{1,0:T(8,128)S(1)} %convolution_subtract_fusion.1, ...), kind=kOutput, calls=%fused_computation.58 | convolution fusion | flops 908328192 | bytes 6294528 | tf_op jit(solution)/shard_map/dot_general | solution.py:11
  168.0 11.7 %all-to-all-start.1 = ((f32[128,1,1024]{2,1,0:T(1,128)}), f32[128,1,1024]{2,1,0:T(1,128)}, u32[]{:S(2)}, u32[]{:S(2)}) async-start(f32[128,1,1024]{2,1,0:T(1,128)} %broadcast_in_dim.71), calls=%async_computation.1 | async-start | bytes 1048576 | tf_op jit(solution)/shard_map/all_to_all | solution.py:33
  182.7 2.6 %collective-permute-start.20 = (f32[512,256]{1,0:T(8,128)}, f32[512,256]{1,0:T(8,128)}, u32[]{:S(2)}, u32[]{:S(2)}) collective-permute-start(f32[512,256]{1,0:T(8,128)} %pad_maximum_fusion.14), channel_id=1, source_target_pairs={{1,0},{2,1},{3,2},{0,3},{5,4},{6,5},{7,6},{4,7},{9,8},{10,9},{11,1... | collective-permute-start | bytes 1572872 | tf_op jit(solution)/shard_map/ppermute | solution.py:26
  187.3 3.1 %collective-permute-start.19 = (f32[512,256]{1,0:T(8,128)}, f32[512,256]{1,0:T(8,128)}, u32[]{:S(2)}, u32[]{:S(2)}) collective-permute-start(f32[512,256]{1,0:T(8,128)} %pad_maximum_fusion.13), channel_id=1, source_target_pairs={{4,0},{8,4},{12,8},{16,12},{20,16},{24,20},{28,24},{32,28},{36,32}... | collective-permute-start | bytes 1572872 | tf_op jit(solution)/shard_map/ppermute | solution.py:21
  190.4 3.1 %all-to-all-done.1 = f32[128,1,1024]{2,1,0:T(1,128)} async-done(((f32[128,1,1024]{2,1,0:T(1,128)}), f32[128,1,1024]{2,1,0:T(1,128)}, u32[]{:S(2)}, u32[]{:S(2)}) %all-to-all-start.1) | async-done | bytes 524320 | tf_op jit(solution)/shard_map/all_to_all | solution.py:33
  196.3 2.5 %collective-permute-done.20 = f32[512,256]{1,0:T(8,128)} collective-permute-done((f32[512,256]{1,0:T(8,128)}, f32[512,256]{1,0:T(8,128)}, u32[]{:S(2)}, u32[]{:S(2)}) %collective-permute-start.20) | collective-permute-done | bytes 524320 | tf_op jit(solution)/shard_map/ppermute | solution.py:26
  198.7 2.0 collective-permute-done.21
  200.8 11.8 %collective-permute-done.22 = f32[512,256]{1,0:T(8,128)} collective-permute-done((f32[512,256]{1,0:T(8,128)}, f32[512,256]{1,0:T(8,128)}, u32[]{:S(2)}, u32[]{:S(2)}) %collective-permute-start.22) | collective-permute-done | bytes 524320 | tf_op jit(solution)/shard_map/ppermute | solution.py:26
  214.0 2.0 fusion.21
  216.1 2.7 %slice_add_fusion = (f32[256,256]{1,0:T(8,128)}, f32[256,256]{1,0:T(8,128)}, f32[256,256]{1,0:T(8,128)}) fusion(f32[1024,256]{1,0:T(8,128)} %get-tuple-element.30, f32[1024,256]{1,0:T(8,128)} %get-tuple-element.31, f32[1024,256]{1,0:T(8,128)} %copy-done.44, f32[1024,256]{1,0:T(8,128)S(1)} %get-tuple-element.37, f32[256]{0:T(256)S(1)} %bitcast.72, ...), kind=kLoop, calls=%fused_computation.87 | loop fusion | flops 1310720 | bytes 3936260 | tf_op jit(solution)/shard_map/add | solution.py:211
  (222 shorter events, 67.8 us)
Async XLA Ops:
  3.1 81.3 %copy-start.3 = (f32[256,256]{1,0:T(8,128)}, f32[256,256]{1,0:T(8,128)S(1)}, u32[]{:S(2)}) copy-start(f32[256,256]{1,0:T(8,128)S(1)} %broadcast_multiply_fusion.5) | copy-start | bytes 786436
  5.1 20.2 %collective-permute-start.2 = (f32[520,256]{1,0:T(8,128)}, f32[520,256]{1,0:T(8,128)}, u32[]{:S(2)}, u32[]{:S(2)}) collective-permute-start(f32[520,256]{1,0:T(8,128)} %maximum_maximum_fusion), channel_id=1, source_target_pairs={{3,0},{0,1},{1,2},{2,3},{7,4},{4,5},{5,6},{6,7},{11,8},{8,9},{9,10... | collective-permute-start | bytes 1597448 | tf_op jit(solution)/shard_map/ppermute | solution.py:26
  7.2 21.9 %collective-permute-start.1 = (f32[520,256]{1,0:T(8,128)}, f32[520,256]{1,0:T(8,128)}, u32[]{:S(2)}, u32[]{:S(2)}) collective-permute-start(f32[520,256]{1,0:T(8,128)} %maximum_maximum_fusion), channel_id=1, source_target_pairs={{1,0},{2,1},{3,2},{0,3},{5,4},{6,5},{7,6},{4,7},{9,8},{10,9},{11,1... | collective-permute-start | bytes 1597448 | tf_op jit(solution)/shard_map/ppermute | solution.py:26
  10.4 23.8 %collective-permute-start = (f32[256,256]{1,0:T(8,128)}, f32[256,256]{1,0:T(8,128)}, u32[]{:S(2)}, u32[]{:S(2)}) collective-permute-start(f32[256,256]{1,0:T(8,128)} %broadcast_multiply_fusion.7), channel_id=1, source_target_pairs={{0,4},{4,8},{8,12},{12,16},{16,20},{20,24},{24,28},{28,32},{32,36}... | collective-permute-start | bytes 786440 | tf_op jit(solution)/shard_map/ppermute | solution.py:21
  28.9 10.6 %collective-permute-start.3 = (f32[256,256]{1,0:T(8,128)}, f32[256,256]{1,0:T(8,128)}, u32[]{:S(2)}, u32[]{:S(2)}) collective-permute-start(f32[256,256]{1,0:T(8,128)} %get-tuple-element.58), channel_id=1, source_target_pairs={{3,0},{0,1},{1,2},{2,3},{7,4},{4,5},{5,6},{6,7},{11,8},{8,9},{9,10... | collective-permute-start | bytes 786440 | tf_op jit(solution)/shard_map/ppermute | solution.py:26
  30.8 8.7 %collective-permute-start.4 = (f32[264,256]{1,0:T(8,128)}, f32[264,256]{1,0:T(8,128)}, u32[]{:S(2)}, u32[]{:S(2)}) collective-permute-start(f32[264,256]{1,0:T(8,128)} %slice.342), channel_id=1, source_target_pairs={{1,0},{2,1},{3,2},{0,3},{5,4},{6,5},{7,6},{4,7},{9,8},{10,9},{11,1... | collective-permute-start | bytes 811016 | tf_op jit(solution)/shard_map/ppermute | solution.py:26
  44.1 49.7 %copy-start.23 = (f32[256,256]{1,0:T(8,128)}, f32[256,256]{1,0:T(8,128)S(1)}, u32[]{:S(2)}) copy-start(f32[256,256]{1,0:T(8,128)S(1)} %broadcast_multiply_fusion.3) | copy-start | bytes 786436
  49.4 10.4 %collective-permute-start.5 = (f32[256,256]{1,0:T(8,128)S(1)}, f32[256,256]{1,0:T(8,128)S(1)}, u32[]{:S(2)}, u32[]{:S(2)}) collective-permute-start(f32[256,256]{1,0:T(8,128)S(1)} %get-tuple-element.51), channel_id=1, source_target_pairs={{4,0},{8,4},{12,8},{16,12},{20,16},{24,20},{28,24},{32,28},{36,32}... | collective-permute-start | bytes 786440 | tf_op jit(solution)/shard_map/ppermute | solution.py:21
  51.3 8.5 %collective-permute-start.6 = (f32[256,256]{1,0:T(8,128)S(1)}, f32[256,256]{1,0:T(8,128)S(1)}, u32[]{:S(2)}, u32[]{:S(2)}) collective-permute-start(f32[256,256]{1,0:T(8,128)S(1)} %get-tuple-element.52), channel_id=1, source_target_pairs={{0,4},{4,8},{8,12},{12,16},{16,20},{20,24},{24,28},{28,32},{32,36}... | collective-permute-start | bytes 786440 | tf_op jit(solution)/shard_map/ppermute | solution.py:21
  55.2 23.7 %collective-permute-start.10 = (f32[512,256]{1,0:T(8,128)S(1)}, f32[512,256]{1,0:T(8,128)S(1)}, u32[]{:S(2)}, u32[]{:S(2)}) collective-permute-start(f32[512,256]{1,0:T(8,128)S(1)} %copy-done.55), channel_id=1, source_target_pairs={{1,0},{2,1},{3,2},{0,3},{5,4},{6,5},{7,6},{4,7},{9,8},{10,9},{11,1... | collective-permute-start | bytes 1572872 | tf_op jit(solution)/shard_map/ppermute | solution.py:26
  58.1 20.7 %collective-permute-start.11 = (f32[512,256]{1,0:T(8,128)S(1)}, f32[512,256]{1,0:T(8,128)S(1)}, u32[]{:S(2)}, u32[]{:S(2)}) collective-permute-start(f32[512,256]{1,0:T(8,128)S(1)} %copy-done.55), channel_id=1, source_target_pairs={{3,0},{0,1},{1,2},{2,3},{7,4},{4,5},{5,6},{6,7},{11,8},{8,9},{9,10... | collective-permute-start | bytes 1572872 | tf_op jit(solution)/shard_map/ppermute | solution.py:26
  58.1 32.0 %copy-start.8 = (f32[256,256]{1,0:T(8,128)S(1)}, f32[256,256]{1,0:T(8,128)}, u32[]{:S(2)}) copy-start(f32[256,256]{1,0:T(8,128)} %param.16) | copy-start | bytes 786436
  58.1 32.0 %copy-start.28 = (f32[256,256]{1,0:T(8,128)S(1)}, f32[256,256]{1,0:T(8,128)}, u32[]{:S(2)}) copy-start(f32[256,256]{1,0:T(8,128)} %copy-done.27) | copy-start | bytes 786436
  58.1 32.0 %copy-start.30 = (f32[256,256]{1,0:T(8,128)S(1)}, f32[256,256]{1,0:T(8,128)}, u32[]{:S(2)}) copy-start(f32[256,256]{1,0:T(8,128)} %get-tuple-element.55) | copy-start | bytes 786436
  58.1 32.0 %copy-start.33 = (f32[256,256]{1,0:T(8,128)S(1)}, f32[256,256]{1,0:T(8,128)}, u32[]{:S(2)}) copy-start(f32[256,256]{1,0:T(8,128)} %slice.269) | copy-start | bytes 786436
  58.1 32.0 %copy-start.43 = (f32[256,256]{1,0:T(8,128)S(1)}, f32[256,256]{1,0:T(8,128)}, u32[]{:S(2)}) copy-start(f32[256,256]{1,0:T(8,128)} %copy-done.42) | copy-start | bytes 786436
  59.9 21.9 %collective-permute-start.7 = (f32[256,256]{1,0:T(8,128)S(1)}, f32[256,256]{1,0:T(8,128)S(1)}, u32[]{:S(2)}, u32[]{:S(2)}) collective-permute-start(f32[256,256]{1,0:T(8,128)S(1)} %get-tuple-element.50), channel_id=1, source_target_pairs={{1,0},{2,1},{3,2},{0,3},{5,4},{6,5},{7,6},{4,7},{9,8},{10,9},{11,1... | collective-permute-start | bytes 786440 | tf_op jit(solution)/shard_map/ppermute | solution.py:26
  62.6 19.2 %collective-permute-start.8 = (f32[256,256]{1,0:T(8,128)S(1)}, f32[256,256]{1,0:T(8,128)S(1)}, u32[]{:S(2)}, u32[]{:S(2)}) collective-permute-start(f32[256,256]{1,0:T(8,128)S(1)} %get-tuple-element.50), channel_id=1, source_target_pairs={{2,0},{3,1},{0,2},{1,3},{6,4},{7,5},{4,6},{5,7},{10,8},{11,9},{8,1... | collective-permute-start | bytes 786440 | tf_op jit(solution)/shard_map/ppermute | solution.py:26
  62.6 21.7 %collective-permute-start.9 = (f32[256,256]{1,0:T(8,128)S(1)}, f32[256,256]{1,0:T(8,128)S(1)}, u32[]{:S(2)}, u32[]{:S(2)}) collective-permute-start(f32[256,256]{1,0:T(8,128)S(1)} %get-tuple-element.50), channel_id=1, source_target_pairs={{3,0},{0,1},{1,2},{2,3},{7,4},{4,5},{5,6},{6,7},{11,8},{8,9},{9,10... | collective-permute-start | bytes 786440 | tf_op jit(solution)/shard_map/ppermute | solution.py:26
  78.8 10.5 %collective-permute-start.12 = (f32[256,256]{1,0:T(8,128)S(1)}, f32[256,256]{1,0:T(8,128)S(1)}, u32[]{:S(2)}, u32[]{:S(2)}) collective-permute-start(f32[256,256]{1,0:T(8,128)S(1)} %get-tuple-element.66), channel_id=1, source_target_pairs={{3,0},{0,1},{1,2},{2,3},{7,4},{4,5},{5,6},{6,7},{11,8},{8,9},{9,10... | collective-permute-start | bytes 786440 | tf_op jit(solution)/shard_map/ppermute | solution.py:26
  78.9 10.7 %collective-permute-start.13 = (f32[256,256]{1,0:T(8,128)S(1)}, f32[256,256]{1,0:T(8,128)S(1)}, u32[]{:S(2)}, u32[]{:S(2)}) collective-permute-start(f32[256,256]{1,0:T(8,128)S(1)} %slice.356), channel_id=1, source_target_pairs={{1,0},{2,1},{3,2},{0,3},{5,4},{6,5},{7,6},{4,7},{9,8},{10,9},{11,1... | collective-permute-start | bytes 786440 | tf_op jit(solution)/shard_map/ppermute | solution.py:26
  102.2 18.6 %collective-permute-start.14 = (f32[256,256]{1,0:T(8,128)}, f32[256,256]{1,0:T(8,128)}, u32[]{:S(2)}, u32[]{:S(2)}) collective-permute-start(f32[256,256]{1,0:T(8,128)} %get-tuple-element.46), channel_id=1, source_target_pairs={{4,0},{8,4},{12,8},{16,12},{20,16},{24,20},{28,24},{32,28},{36,32}... | collective-permute-start | bytes 786440 | tf_op jit(solution)/shard_map/ppermute | solution.py:21
  104.5 16.4 %collective-permute-start.15 = (f32[256,256]{1,0:T(8,128)}, f32[256,256]{1,0:T(8,128)}, u32[]{:S(2)}, u32[]{:S(2)}) collective-permute-start(f32[256,256]{1,0:T(8,128)} %get-tuple-element.47), channel_id=1, source_target_pairs={{0,4},{4,8},{8,12},{12,16},{16,20},{20,24},{24,28},{28,32},{32,36}... | collective-permute-start | bytes 786440 | tf_op jit(solution)/shard_map/ppermute | solution.py:21
  108.8 22.6 %all-to-all-start = ((f32[128,1,768]{2,1,0:T(1,128)}), f32[128,1,768]{2,1,0:T(1,128)}, u32[]{:S(2)}, u32[]{:S(2)}) async-start(f32[128,1,768]{2,1,0:T(1,128)} %broadcast_in_dim.64), calls=%async_computation | async-start | bytes 786432 | tf_op jit(solution)/shard_map/all_to_all | solution.py:33
  124.8 25.0 %collective-permute-start.16 = (f32[512,256]{1,0:T(8,128)}, f32[512,256]{1,0:T(8,128)}, u32[]{:S(2)}, u32[]{:S(2)}) collective-permute-start(f32[512,256]{1,0:T(8,128)} %pad_maximum_fusion.12), channel_id=1, source_target_pairs={{1,0},{2,1},{3,2},{0,3},{5,4},{6,5},{7,6},{4,7},{9,8},{10,9},{11,1... | collective-permute-start | bytes 1572872 | tf_op jit(solution)/shard_map/ppermute | solution.py:26
  127.5 23.3 %collective-permute-start.17 = (f32[512,256]{1,0:T(8,128)}, f32[512,256]{1,0:T(8,128)}, u32[]{:S(2)}, u32[]{:S(2)}) collective-permute-start(f32[512,256]{1,0:T(8,128)} %pad_maximum_fusion.12), channel_id=1, source_target_pairs={{2,0},{3,1},{0,2},{1,3},{6,4},{7,5},{4,6},{5,7},{10,8},{11,9},{8,1... | collective-permute-start | bytes 1572872 | tf_op jit(solution)/shard_map/ppermute | solution.py:26
  128.0 26.4 %collective-permute-start.18 = (f32[512,256]{1,0:T(8,128)}, f32[512,256]{1,0:T(8,128)}, u32[]{:S(2)}, u32[]{:S(2)}) collective-permute-start(f32[512,256]{1,0:T(8,128)} %pad_maximum_fusion.12), channel_id=1, source_target_pairs={{3,0},{0,1},{1,2},{2,3},{7,4},{4,5},{5,6},{6,7},{11,8},{8,9},{9,10... | collective-permute-start | bytes 1572872 | tf_op jit(solution)/shard_map/ppermute | solution.py:26
  168.0 25.6 %all-to-all-start.1 = ((f32[128,1,1024]{2,1,0:T(1,128)}), f32[128,1,1024]{2,1,0:T(1,128)}, u32[]{:S(2)}, u32[]{:S(2)}) async-start(f32[128,1,1024]{2,1,0:T(1,128)} %broadcast_in_dim.71), calls=%async_computation.1 | async-start | bytes 1048576 | tf_op jit(solution)/shard_map/all_to_all | solution.py:33
  182.7 16.0 %collective-permute-start.20 = (f32[512,256]{1,0:T(8,128)}, f32[512,256]{1,0:T(8,128)}, u32[]{:S(2)}, u32[]{:S(2)}) collective-permute-start(f32[512,256]{1,0:T(8,128)} %pad_maximum_fusion.14), channel_id=1, source_target_pairs={{1,0},{2,1},{3,2},{0,3},{5,4},{6,5},{7,6},{4,7},{9,8},{10,9},{11,1... | collective-permute-start | bytes 1572872 | tf_op jit(solution)/shard_map/ppermute | solution.py:26
  185.3 15.4 %collective-permute-start.21 = (f32[512,256]{1,0:T(8,128)}, f32[512,256]{1,0:T(8,128)}, u32[]{:S(2)}, u32[]{:S(2)}) collective-permute-start(f32[512,256]{1,0:T(8,128)} %pad_maximum_fusion.14), channel_id=1, source_target_pairs={{2,0},{3,1},{0,2},{1,3},{6,4},{7,5},{4,6},{5,7},{10,8},{11,9},{8,1... | collective-permute-start | bytes 1572872 | tf_op jit(solution)/shard_map/ppermute | solution.py:26
  185.9 26.7 %collective-permute-start.22 = (f32[512,256]{1,0:T(8,128)}, f32[512,256]{1,0:T(8,128)}, u32[]{:S(2)}, u32[]{:S(2)}) collective-permute-start(f32[512,256]{1,0:T(8,128)} %pad_maximum_fusion.14), channel_id=1, source_target_pairs={{3,0},{0,1},{1,2},{2,3},{7,4},{4,5},{5,6},{6,7},{11,8},{8,9},{9,10... | collective-permute-start | bytes 1572872 | tf_op jit(solution)/shard_map/ppermute | solution.py:26
  187.3 28.7 %collective-permute-start.19 = (f32[512,256]{1,0:T(8,128)}, f32[512,256]{1,0:T(8,128)}, u32[]{:S(2)}, u32[]{:S(2)}) collective-permute-start(f32[512,256]{1,0:T(8,128)} %pad_maximum_fusion.13), channel_id=1, source_target_pairs={{4,0},{8,4},{12,8},{16,12},{20,16},{24,20},{28,24},{32,28},{36,32}... | collective-permute-start | bytes 1572872 | tf_op jit(solution)/shard_map/ppermute | solution.py:21
  (51 other events, 866.9 us)
